TPU v7x, 32 devices: a whole 2x2x4 slice. The times are simulated.
32 devices in a mesh: outer: 8 (over z, y), inner: 4 (over x, core).
Axes of the slice: x: 2, y: 2, z: 4, core: 2. Of those that a mesh axis runs over, the one named last changes fastest.
Arguments:
- queries: bfloat16 [8192, 1536], P(('outer', 'inner')), may hold values from -8 to 8
- key_rows: bfloat16 [8192, 1536], P(('outer', 'inner')), may hold values from -8 to 8
- value_rows: bfloat16 [8192, 1536], P(('outer', 'inner')), may hold values from -6 to 6
- upstream: bfloat16 [8192, 1536], P(('outer', 'inner')), may hold values from -6 to 6
- short_offsets: int32 [16], replicated, may hold values from 0 to 1
- global_offsets: int32 [16], replicated, may hold values from 0 to 15
Outputs:
- grad_queries: bfloat16 [8192, 1536], P(('outer', 'inner'))
- grad_keys: bfloat16 [8192, 1536], P(('outer', 'inner'))
- grad_values: bfloat16 [8192, 1536], P(('outer', 'inner'))
All inputs are finite; a program needn't handle non-finite values.
Results may differ from a plain program's by a relative error of at most 0.006.
The roundings to bfloat16 on the way count: a program that leaves them out, or rounds other values in their place, can miss the bound.
Values may be sent and summed in bfloat16 or wider, within the bound.
A program may use at most 128 MiB of HBM per device.

v0:
```python
import jax
import jax.numpy as jnp
from jax import lax
from jax.sharding import PartitionSpec as P

H = 16
HD = 96
D = 1536
TOK_DEV = 256
KEEP_A = 512
KEEP_B = 512


def pick_rows(block, offsets, stride):
    count = block.shape[0] // stride
    shaped = block.reshape(count, stride, H, HD)
    onehot = (jnp.arange(stride, dtype=jnp.int32)[:, None] == offsets[None, :]).astype(block.dtype)
    return jnp.sum(shaped * onehot[None, :, :, None], axis=1)


def put_rows(grads, offsets, stride):
    onehot = (jnp.arange(stride, dtype=jnp.int32)[:, None] == offsets[None, :]).astype(jnp.float32)
    spread = grads[:, None, :, :] * onehot[None, :, :, None]
    return spread.reshape(grads.shape[0] * stride, H * HD)


def as_heads(flat):
    return flat.reshape(flat.shape[0], H, HD)


def attend_back(query_part, key_part, value_part, grad_part):
    softmax_scale = HD ** (-0.5)
    scores = (
        jnp.einsum("qhd,khd->hqk", query_part, key_part, preferred_element_type=jnp.float32)
        * softmax_scale
    )
    row_max = jnp.max(scores, axis=-1, keepdims=True)
    weights = jnp.exp(scores - row_max)
    probs = weights / jnp.sum(weights, axis=-1, keepdims=True)
    probs_low = probs.astype(jnp.bfloat16)
    output = jnp.einsum("hqk,khd->qhd", probs_low, value_part, preferred_element_type=jnp.float32)
    delta = jnp.sum(grad_part.astype(jnp.float32) * output, axis=-1)
    dprobs = jnp.einsum("qhd,khd->hqk", grad_part, value_part, preferred_element_type=jnp.float32)
    dscores = (probs * (dprobs - jnp.transpose(delta)[:, :, None])).astype(jnp.bfloat16)
    grad_q = (
        jnp.einsum("hqk,khd->qhd", dscores, key_part, preferred_element_type=jnp.float32)
        * softmax_scale
    )
    grad_k = (
        jnp.einsum("hqk,qhd->khd", dscores, query_part, preferred_element_type=jnp.float32)
        * softmax_scale
    )
    grad_v = jnp.einsum("hqk,qhd->khd", probs_low, grad_part, preferred_element_type=jnp.float32)
    return (grad_q, grad_k, grad_v)


def grouped_back(query_part, key_part, value_part, grad_part):
    head_groups = 4

    def split_heads(member):
        return jnp.moveaxis(
            member.reshape(member.shape[0], head_groups, H // head_groups, HD), 1, 0
        )

    def single_group(pack):
        return attend_back(pack[0], pack[1], pack[2], pack[3])

    mapped = lax.map(
        single_group,
        (
            split_heads(query_part),
            split_heads(key_part),
            split_heads(value_part),
            split_heads(grad_part),
        ),
    )
    return [jnp.moveaxis(member, 0, 1).reshape(member.shape[1], H, HD) for member in mapped]


def local(queries, key_rows, value_rows, upstream, short_offsets, global_offsets):
    inner_size = lax.axis_size("inner")
    all_size = lax.axis_size(("outer", "inner"))
    short_stride = TOK_DEV * inner_size // KEEP_A
    far_count = KEEP_B // all_size
    far_stride = TOK_DEV // far_count
    near = [
        pick_rows(member, short_offsets, short_stride)
        for member in (queries, key_rows, value_rows, upstream)
    ]
    split = (
        lax.all_to_all(near[0], "inner", split_axis=1, concat_axis=0, tiled=True),
        lax.all_to_all(near[1], "inner", split_axis=1, concat_axis=0, tiled=True),
        lax.all_to_all(near[2], "inner", split_axis=1, concat_axis=0, tiled=True),
        lax.all_to_all(near[3], "inner", split_axis=1, concat_axis=0, tiled=True),
    )
    head_results = attend_back(split[0], split[1], split[2], split[3])
    back = (
        lax.all_to_all(head_results[0], "inner", split_axis=0, concat_axis=1, tiled=True),
        lax.all_to_all(head_results[1], "inner", split_axis=0, concat_axis=1, tiled=True),
        lax.all_to_all(head_results[2], "inner", split_axis=0, concat_axis=1, tiled=True),
    )
    near_final = [back[0], back[1], back[2]]
    far = [
        pick_rows(member, global_offsets, far_stride).reshape(far_count, D)
        for member in (queries, key_rows, value_rows, upstream)
    ]
    gathered = (
        lax.all_gather(far[0], ("outer", "inner"), axis=0, tiled=True),
        lax.all_gather(far[1], ("outer", "inner"), axis=0, tiled=True),
        lax.all_gather(far[2], ("outer", "inner"), axis=0, tiled=True),
        lax.all_gather(far[3], ("outer", "inner"), axis=0, tiled=True),
    )
    whole_grads = grouped_back(
        as_heads(gathered[0]), as_heads(gathered[1]), as_heads(gathered[2]), as_heads(gathered[3])
    )
    start = lax.axis_index(("outer", "inner")) * far_count
    far_final = [lax.dynamic_slice_in_dim(member, start, far_count, 0) for member in whole_grads]
    results = []
    for index in range(3):
        total = put_rows(near_final[index], short_offsets, short_stride) + put_rows(
            far_final[index], global_offsets, far_stride
        )
        results.append(total.astype(jnp.bfloat16))
    return (results[0], results[1], results[2])


def solution(mesh):
    in_specs = (
        P(("outer", "inner"), None),
        P(("outer", "inner"), None),
        P(("outer", "inner"), None),
        P(("outer", "inner"), None),
        P(),
        P(),
    )
    out_specs = (
        P(("outer", "inner"), None),
        P(("outer", "inner"), None),
        P(("outer", "inner"), None),
    )
    return jax.shard_map(local, mesh=mesh, in_specs=in_specs, out_specs=out_specs, check_vma=False)
```

profile of v0, /device:TPU:1, one launch (start us, length us, event | category | flops | bytes accessed | tf_op | source)
XLA Modules:
  0.0 338.5 jit_solution(16568514531735868120)
XLA Ops:
  15.6 3.2 multiply_reduce_fusion.2
  29.6 4.7 %multiply_reduce_fusion.7 = (bf16[128,16,96]{2,1,0:T(8,128)(2,1)}, bf16[128,16,96]{2,1,0:T(8,128)(2,1)}, bf16[128,16,96]{2,1,0:T(8,128)(2,1)}, bf16[128,16,96]{2,1,0:T(8,128)(2,1)}) fusion(bf16[128,2,16,96]{3,2,1,0:T(8,128)(2,1)} %reshape.172, bf16[2,16]{1,0:T(2,128)(2,1)S(1)} %get-tuple-element.84, bf16[128,2,16,96]{3,2,1,0:T(8,128)(2,1)S(1)} %reshape.171, ...), kind=kLoop, calls=%fused_computation.79 | loop fusion | flops 2359296 | bytes 4718656 | tf_op jit(solution)/shard_map/reduce_sum | solution.py:18
  36.7 4.3 %all-to-all-start.1 = ((bf16[128,16,96]{0,2,1:T(8,128)(2,1)}), bf16[128,16,96]{0,2,1:T(8,128)(2,1)S(1)}, u32[]{:S(2)}, u32[]{:S(2)}) async-start(bf16[128,16,96]{0,2,1:T(8,128)(2,1)} %copy.120), calls=%async_computation.1 | async-start | bytes 786432 | tf_op jit(solution)/shard_map/all_to_all | solution.py:91
  43.1 4.2 %all-to-all-done.1 = bf16[128,16,96]{0,2,1:T(8,128)(2,1)S(1)} async-done(((bf16[128,16,96]{0,2,1:T(8,128)(2,1)}), bf16[128,16,96]{0,2,1:T(8,128)(2,1)S(1)}, u32[]{:S(2)}, u32[]{:S(2)}) %all-to-all-start.1) | async-done | bytes 393248 | tf_op jit(solution)/shard_map/all_to_all | solution.py:91
  47.3 4.5 %all-to-all-start = ((bf16[128,16,96]{0,2,1:T(8,128)(2,1)}), bf16[128,16,96]{0,2,1:T(8,128)(2,1)S(1)}, u32[]{:S(2)}, u32[]{:S(2)}) async-start(bf16[128,16,96]{0,2,1:T(8,128)(2,1)} %copy.118), calls=%async_computation | async-start | bytes 786432 | tf_op jit(solution)/shard_map/all_to_all | solution.py:92
  55.0 3.4 %all-to-all-done = bf16[128,16,96]{0,2,1:T(8,128)(2,1)S(1)} async-done(((bf16[128,16,96]{0,2,1:T(8,128)(2,1)}), bf16[128,16,96]{0,2,1:T(8,128)(2,1)S(1)}, u32[]{:S(2)}, u32[]{:S(2)}) %all-to-all-start) | async-done | bytes 393248 | tf_op jit(solution)/shard_map/all_to_all | solution.py:92
  58.4 4.3 %all-to-all-start.2 = ((bf16[128,16,96]{0,2,1:T(8,128)(2,1)}), bf16[128,16,96]{0,2,1:T(8,128)(2,1)S(1)}, u32[]{:S(2)}, u32[]{:S(2)}) async-start(bf16[128,16,96]{0,2,1:T(8,128)(2,1)} %copy.122), calls=%async_computation.2 | async-start | bytes 786432 | tf_op jit(solution)/shard_map/all_to_all | solution.py:94
  62.7 3.5 %fusion.113 = (f32[4,512]{1,0:T(4,128)S(1)}, f32[4,512,512]{1,2,0:T(8,128)}) fusion(bf16[4,4,12,8,128]{4,3,2,1,0:T(8,128)(2,1)S(1)} %bitcast.233, bf16[4,4,12,8,128]{4,3,2,1,0:T(8,128)(2,1)S(1)} %bitcast.235), kind=kOutput, calls=%fused_computation.115 | convolution fusion | flops 204472832 | bytes 4988928 | tf_op jit(solution)/shard_map/sub | solution.py:38
  71.8 4.5 %all-to-all-start.3 = ((bf16[128,16,96]{0,2,1:T(8,128)(2,1)}), bf16[128,16,96]{0,2,1:T(8,128)(2,1)}, u32[]{:S(2)}, u32[]{:S(2)}) async-start(bf16[128,16,96]{0,2,1:T(8,128)(2,1)} %copy.124), calls=%async_computation.3 | async-start | bytes 786432 | tf_op jit(solution)/shard_map/all_to_all | solution.py:93
  79.4 3.6 %all-to-all-done.3 = bf16[128,16,96]{0,2,1:T(8,128)(2,1)} async-done(((bf16[128,16,96]{0,2,1:T(8,128)(2,1)}), bf16[128,16,96]{0,2,1:T(8,128)(2,1)}, u32[]{:S(2)}, u32[]{:S(2)}) %all-to-all-start.3) | async-done | bytes 393248 | tf_op jit(solution)/shard_map/all_to_all | solution.py:93
  83.0 4.4 %all-to-all-start.6 = ((f32[512,4,96]{2,1,0:T(4,128)}), f32[512,4,96]{2,1,0:T(4,128)S(1)}, u32[]{:S(2)}, u32[]{:S(2)}) async-start(f32[512,4,96]{2,1,0:T(4,128)} %copy.145), calls=%async_computation.6 | async-start | bytes 2097152 | tf_op jit(solution)/shard_map/all_to_all | solution.py:100
  96.0 5.3 %all-to-all-done.6 = f32[512,4,96]{2,1,0:T(4,128)S(1)} async-done(((f32[512,4,96]{2,1,0:T(4,128)}), f32[512,4,96]{2,1,0:T(4,128)S(1)}, u32[]{:S(2)}, u32[]{:S(2)}) %all-to-all-start.6) | async-done | bytes 786464 | tf_op jit(solution)/shard_map/all_to_all | solution.py:100
  101.3 5.1 %all-to-all-start.4 = ((f32[512,4,96]{2,1,0:T(4,128)}), f32[512,4,96]{2,1,0:T(4,128)}, u32[]{:S(2)}, u32[]{:S(2)}) async-start(f32[512,4,96]{2,1,0:T(4,128)} %copy.129), calls=%async_computation.4 | async-start | bytes 2097152 | tf_op jit(solution)/shard_map/all_to_all | solution.py:98
  110.5 9.6 %all-to-all-done.4 = f32[512,4,96]{2,1,0:T(4,128)} async-done(((f32[512,4,96]{2,1,0:T(4,128)}), f32[512,4,96]{2,1,0:T(4,128)}, u32[]{:S(2)}, u32[]{:S(2)}) %all-to-all-start.4) | async-done | bytes 786464 | tf_op jit(solution)/shard_map/all_to_all | solution.py:98
  120.1 4.4 %all-to-all-start.5 = ((f32[512,4,96]{2,1,0:T(4,128)}), f32[512,4,96]{2,1,0:T(4,128)S(1)}, u32[]{:S(2)}, u32[]{:S(2)}) async-start(f32[512,4,96]{2,1,0:T(4,128)} %copy.139), calls=%async_computation.5 | async-start | bytes 2097152 | tf_op jit(solution)/shard_map/all_to_all | solution.py:99
  128.3 9.8 %all-to-all-done.5 = f32[512,4,96]{2,1,0:T(4,128)S(1)} async-done(((f32[512,4,96]{2,1,0:T(4,128)}), f32[512,4,96]{2,1,0:T(4,128)S(1)}, u32[]{:S(2)}, u32[]{:S(2)}) %all-to-all-start.5) | async-done | bytes 786464 | tf_op jit(solution)/shard_map/all_to_all | solution.py:99
  139.8 4.6 %broadcast_multiply_fusion.1 = (f32[128,2,16,96]{3,2,1,0:T(8,128)}, f32[128,2,16,96]{3,2,1,0:T(8,128)}, f32[128,2,16,96]{3,2,1,0:T(8,128)S(1)}) fusion(f32[128,16,96]{2,1,0:T(8,128)S(1)} %copy.148, f32[2,16]{1,0:T(2,128)S(1)} %copy-done.15, f32[128,16,96]{2,1,0:T(8,128)} %copy.142, f32[128,16,96]{2,1,0:T(8,128)} %copy.132), kind=kLoop, calls=%fused_computation.69 | loop fusion | flops 1179648 | bytes 7078016 | tf_op jit(solution)/shard_map/mul | solution.py:23
  157.0 34.7 %all-gather.9.cloned.1.call-done = bf16[512,1536]{1,0:T(8,128)(2,1)} async-done(((bf16[16,1536]{1,0:T(8,128)(2,1)}), bf16[512,1536]{1,0:T(8,128)(2,1)}) %all-gather.9.cloned.1.call-update) | async-done | bytes 1572880 | tf_op jit(solution)/shard_map/all_gather | solution.py:111
  193.5 54.9 %all-gather.5.cloned.1.call-done = bf16[512,1536]{1,0:T(8,128)(2,1)} async-done(((bf16[16,1536]{1,0:T(8,128)(2,1)}), bf16[512,1536]{1,0:T(8,128)(2,1)}) %all-gather.5.cloned.1.call-update) | async-done | bytes 1572880 | tf_op jit(solution)/shard_map/all_gather | solution.py:109
  250.9 59.4 %while.14 = (s32[]{:T(128)}, f32[4,512,4,96]{1,3,2,0:T(8,128)}, f32[4,512,4,96]{1,3,2,0:T(8,128)}, f32[4,512,4,96]{1,3,2,0:T(8,128)}, bf16[4,512,4,96]{1,3,2,0:T...) while((s32[]{:T(128)}, f32[4,512,4,96]{1,3,2,0:T(8,128)}, ...), condition=%wide.region_15.16_spmd, body=%wide.region_11.15_spmd.sunk | while | flops 1218378240 | bytes 54179996 | solution.py:68
  250.9 4.4 %fusion.160 = (f32[4,512]{1,0:T(4,128)S(1)}, f32[4,512,512]{1,2,0:T(8,128)}) fusion(bf16[4,512,4,96]{1,3,2,0:T(8,128)(2,1)S(1)} %get-tuple-element.166, s32[]{:T(128)S(6)} %copy.234, bf16[4,512,4,96]{1,3,2,0:T(8,128)(2,1)} %get-tuple-element.165), kind=kOutput, calls=%fused_computation.114.clone.1 | convolution fusion | flops 204472832 | bytes 4989952 | tf_op jit(solution)/shard_map/while/body/eval_jaxpr/sub | solution.py:38
  265.7 4.4 %fusion.160 = (f32[4,512]{1,0:T(4,128)S(1)}, f32[4,512,512]{1,2,0:T(8,128)}) fusion(bf16[4,512,4,96]{1,3,2,0:T(8,128)(2,1)S(1)} %get-tuple-element.166, s32[]{:T(128)S(6)} %copy.234, bf16[4,512,4,96]{1,3,2,0:T(8,128)(2,1)} %get-tuple-element.165), kind=kOutput, calls=%fused_computation.114.clone.1 | convolution fusion | flops 204472832 | bytes 4989952 | tf_op jit(solution)/shard_map/while/body/eval_jaxpr/sub | solution.py:38
  280.6 4.4 %fusion.160 = (f32[4,512]{1,0:T(4,128)S(1)}, f32[4,512,512]{1,2,0:T(8,128)}) fusion(bf16[4,512,4,96]{1,3,2,0:T(8,128)(2,1)S(1)} %get-tuple-element.166, s32[]{:T(128)S(6)} %copy.234, bf16[4,512,4,96]{1,3,2,0:T(8,128)(2,1)} %get-tuple-element.165), kind=kOutput, calls=%fused_computation.114.clone.1 | convolution fusion | flops 204472832 | bytes 4989952 | tf_op jit(solution)/shard_map/while/body/eval_jaxpr/sub | solution.py:38
  295.5 4.4 %fusion.160 = (f32[4,512]{1,0:T(4,128)S(1)}, f32[4,512,512]{1,2,0:T(8,128)}) fusion(bf16[4,512,4,96]{1,3,2,0:T(8,128)(2,1)S(1)} %get-tuple-element.166, s32[]{:T(128)S(6)} %copy.234, bf16[4,512,4,96]{1,3,2,0:T(8,128)(2,1)} %get-tuple-element.165), kind=kOutput, calls=%fused_computation.114.clone.1 | convolution fusion | flops 204472832 | bytes 4989952 | tf_op jit(solution)/shard_map/while/body/eval_jaxpr/sub | solution.py:38
  (136 shorter events, 133.7 us)
Async XLA Ops:
  7.2 145.5 %all-gather.11.cloned.1.call-start = ((), (), s32[]{:S(2)}) async-start(), calls=%async_computation.10 | async-start | bytes 1622016 | tf_op jit(solution)/shard_map/all_gather | solution.py:110
  18.8 4.6 %copy-start.7 = (bf16[256,1536]{1,0:T(8,128)(2,1)S(1)}, bf16[256,1536]{1,0:T(8,128)(2,1)}, u32[]{:S(2)}) copy-start(bf16[256,1536]{1,0:T(8,128)(2,1)} %param.9) | copy-start | bytes 2359300
  19.5 135.8 %all-gather.7.cloned.1.call-start = ((), (), s32[]{:S(2)}) async-start(), calls=%async_computation.8 | async-start | bytes 1622016 | tf_op jit(solution)/shard_map/all_gather | solution.py:108
  20.4 171.4 %all-gather.9.cloned.1.call-start = ((), (), s32[]{:S(2)}) async-start(), calls=%async_computation.9 | async-start | bytes 1622016 | tf_op jit(solution)/shard_map/all_gather | solution.py:111
  24.2 4.8 %copy-start.16 = (s32[16]{0:T(128)S(1)}, s32[16]{0:T(128)}, u32[]{:S(2)}) copy-start(s32[16]{0:T(128)} %param.12) | copy-start | bytes 196
  34.4 17.4 %copy-start.14 = (bf16[16,16,96]{2,1,0:T(8,128)(2,1)S(1)}, bf16[16,16,96]{2,1,0:T(8,128)(2,1)}, u32[]{:S(2)}) copy-start(bf16[16,16,96]{2,1,0:T(8,128)(2,1)} %get-tuple-element.53) | copy-start | bytes 147460
  34.4 18.2 %copy-start.9 = (bf16[128,16,96]{2,1,0:T(8,128)(2,1)S(1)}, bf16[128,16,96]{2,1,0:T(8,128)(2,1)}, u32[]{:S(2)}) copy-start(bf16[128,16,96]{2,1,0:T(8,128)(2,1)} %get-tuple-element.54) | copy-start | bytes 1179652
  34.4 19.4 %copy-start.8 = (bf16[128,16,96]{2,1,0:T(8,128)(2,1)S(1)}, bf16[128,16,96]{2,1,0:T(8,128)(2,1)}, u32[]{:S(2)}) copy-start(bf16[128,16,96]{2,1,0:T(8,128)(2,1)} %get-tuple-element.56) | copy-start | bytes 1179652
  36.7 10.7 %all-to-all-start.1 = ((bf16[128,16,96]{0,2,1:T(8,128)(2,1)}), bf16[128,16,96]{0,2,1:T(8,128)(2,1)S(1)}, u32[]{:S(2)}, u32[]{:S(2)}) async-start(bf16[128,16,96]{0,2,1:T(8,128)(2,1)} %copy.120), calls=%async_computation.1 | async-start | bytes 786432 | tf_op jit(solution)/shard_map/all_to_all | solution.py:91
  47.3 11.0 %all-to-all-start = ((bf16[128,16,96]{0,2,1:T(8,128)(2,1)}), bf16[128,16,96]{0,2,1:T(8,128)(2,1)S(1)}, u32[]{:S(2)}, u32[]{:S(2)}) async-start(bf16[128,16,96]{0,2,1:T(8,128)(2,1)} %copy.118), calls=%async_computation | async-start | bytes 786432 | tf_op jit(solution)/shard_map/all_to_all | solution.py:92
  51.8 196.5 %all-gather.5.cloned.1.call-start = ((), (), s32[]{:S(2)}) async-start(), calls=%async_computation.7 | async-start | bytes 1622016 | tf_op jit(solution)/shard_map/all_gather | solution.py:109
  58.4 7.8 %copy-start.10 = (bf16[128,16,96]{0,2,1:T(8,128)(2,1)}, bf16[128,16,96]{0,2,1:T(8,128)(2,1)S(1)}, u32[]{:S(2)}) copy-start(bf16[128,16,96]{0,2,1:T(8,128)(2,1)S(1)} %all-to-all-done) | copy-start | bytes 1179652
  58.4 13.4 %all-to-all-start.2 = ((bf16[128,16,96]{0,2,1:T(8,128)(2,1)}), bf16[128,16,96]{0,2,1:T(8,128)(2,1)S(1)}, u32[]{:S(2)}, u32[]{:S(2)}) async-start(bf16[128,16,96]{0,2,1:T(8,128)(2,1)} %copy.122), calls=%async_computation.2 | async-start | bytes 786432 | tf_op jit(solution)/shard_map/all_to_all | solution.py:94
  71.8 4.6 %copy-start.12 = (bf16[128,16,96]{0,2,1:T(8,128)(2,1)}, bf16[128,16,96]{0,2,1:T(8,128)(2,1)S(1)}, u32[]{:S(2)}) copy-start(bf16[128,16,96]{0,2,1:T(8,128)(2,1)S(1)} %all-to-all-done.2) | copy-start | bytes 1179652
  71.8 11.2 %all-to-all-start.3 = ((bf16[128,16,96]{0,2,1:T(8,128)(2,1)}), bf16[128,16,96]{0,2,1:T(8,128)(2,1)}, u32[]{:S(2)}, u32[]{:S(2)}) async-start(bf16[128,16,96]{0,2,1:T(8,128)(2,1)} %copy.124), calls=%async_computation.3 | async-start | bytes 786432 | tf_op jit(solution)/shard_map/all_to_all | solution.py:93
  83.0 18.3 %all-to-all-start.6 = ((f32[512,4,96]{2,1,0:T(4,128)}), f32[512,4,96]{2,1,0:T(4,128)S(1)}, u32[]{:S(2)}, u32[]{:S(2)}) async-start(f32[512,4,96]{2,1,0:T(4,128)} %copy.145), calls=%async_computation.6 | async-start | bytes 2097152 | tf_op jit(solution)/shard_map/all_to_all | solution.py:100
  89.1 3.1 copy-start.11
  101.3 18.8 %all-to-all-start.4 = ((f32[512,4,96]{2,1,0:T(4,128)}), f32[512,4,96]{2,1,0:T(4,128)}, u32[]{:S(2)}, u32[]{:S(2)}) async-start(f32[512,4,96]{2,1,0:T(4,128)} %copy.129), calls=%async_computation.4 | async-start | bytes 2097152 | tf_op jit(solution)/shard_map/all_to_all | solution.py:98
  120.1 18.0 %all-to-all-start.5 = ((f32[512,4,96]{2,1,0:T(4,128)}), f32[512,4,96]{2,1,0:T(4,128)S(1)}, u32[]{:S(2)}, u32[]{:S(2)}) async-start(f32[512,4,96]{2,1,0:T(4,128)} %copy.139), calls=%async_computation.5 | async-start | bytes 2097152 | tf_op jit(solution)/shard_map/all_to_all | solution.py:99
  128.3 11.5 %copy-start.15 = (f32[2,16]{1,0:T(2,128)S(1)}, f32[2,16]{1,0:T(2,128)}, u32[]{:S(2)}) copy-start(f32[2,16]{1,0:T(2,128)} %get-tuple-element.85) | copy-start | bytes 388
  255.3 3.9 %copy-start = (f32[4,512,512]{1,2,0:T(8,128)S(1)}, f32[4,512,512]{1,2,0:T(8,128)}, u32[]{:S(2)}) copy-start(f32[4,512,512]{1,2,0:T(8,128)} %get-tuple-element.141) | copy-start | bytes 12582916 | tf_op jit(solution)/shard_map/while
  270.2 3.9 %copy-start = (f32[4,512,512]{1,2,0:T(8,128)S(1)}, f32[4,512,512]{1,2,0:T(8,128)}, u32[]{:S(2)}) copy-start(f32[4,512,512]{1,2,0:T(8,128)} %get-tuple-element.141) | copy-start | bytes 12582916 | tf_op jit(solution)/shard_map/while
  285.0 3.9 %copy-start = (f32[4,512,512]{1,2,0:T(8,128)S(1)}, f32[4,512,512]{1,2,0:T(8,128)}, u32[]{:S(2)}) copy-start(f32[4,512,512]{1,2,0:T(8,128)} %get-tuple-element.141) | copy-start | bytes 12582916 | tf_op jit(solution)/shard_map/while
  299.9 3.9 %copy-start = (f32[4,512,512]{1,2,0:T(8,128)S(1)}, f32[4,512,512]{1,2,0:T(8,128)}, u32[]{:S(2)}) copy-start(f32[4,512,512]{1,2,0:T(8,128)} %get-tuple-element.141) | copy-start | bytes 12582916 | tf_op jit(solution)/shard_map/while
  (10 other events, 26.4 us)
Sparse Core Ops, SparseCore 0:
  19.7 58.2 all-gather.10
  80.9 54.1 all-gather.6
  137.9 53.8 all-gather.8
  194.5 53.8 all-gather.4
where the time goes:
time: 340 us; the launch traced here: 338 us
  waiting for transfers between devices  128 us (38%)
  local copies, waits for them, and re-layouts  69.1 us (20%)
  matrix products  58.6 us (17%)
  other arithmetic  36.5 us (11%)
  starting transfers between devices  31.7 us (9%)
  between operations  14 us (4%)
    all_gather x1, waiting for transfers between devices, local(): lax.all_gather(far[1], ('outer', 'inner'), axis=0, tiled=True)  54.9 us
    all_gather x1, waiting for transfers between devices, local(): lax.all_gather(far[3], ('outer', 'inner'), axis=0, tiled=True)  34.7 us
    sub x5, matrix products, attend_back(): weights = jnp.exp(scores - row_max)  21.2 us
    mul x9, local copies, waits for them, and re-layouts, put_rows(): spread = grads[:, None, :, :] * onehot[None, :, :, None]  19.9 us
    reshape x8, local copies, waits for them, and re-layouts, pick_rows(): shaped = block.reshape(count, stride, H, HD)  15.3 us
    convert_element_type x5, other arithmetic, attend_back(): probs_low = probs.astype(jnp.bfloat16)  14.6 us
    dot_general x5, matrix products, attend_back(): jnp.einsum('hqk,khd->qhd', dscores, key_part, preferred_element_type=jnp....  10.8 us
    all_to_all x1, waiting for transfers between devices, local(): lax.all_to_all(head_results[1], 'inner', split_axis=0, concat_axis=1, til...  9.81 us
  transfers between devices with their start and end apart: 11, of which 9 were waited for; matrix products, arithmetic and copies ran while one was open for 20% of the time, Pallas kernels for 0%

commit v1 on v0

v1 whole, which is shorter than its diff:
```python
import functools
import math

import jax
import jax.numpy as jnp
from jax import lax
from jax.experimental import pallas as pl
from jax.experimental.pallas import tpu as pltpu
from jax.sharding import PartitionSpec as P

H = 16
HD = 96
D = 1536
KEEP_A = 512
KEEP_B = 512
LANES = 128
MESH = pl.DeviceIdType.MESH


def pick_rows(block, offsets, stride):
    count = block.shape[0] // stride
    shaped = block.reshape(count, stride, H, HD)
    onehot = (jnp.arange(stride, dtype=jnp.int32)[:, None] == offsets[None, :]).astype(block.dtype)
    return jnp.sum(shaped * onehot[None, :, :, None], axis=1)


def put_rows(grads, offsets, stride):
    onehot = (jnp.arange(stride, dtype=jnp.int32)[:, None] == offsets[None, :]).astype(jnp.float32)
    spread = grads[:, None, :, :] * onehot[None, :, :, None]
    return spread.reshape(grads.shape[0] * stride, H * HD)


def attend_back(query_part, key_part, value_part, grad_part):
    softmax_scale = HD ** (-0.5)
    scores = (
        jnp.einsum("qhd,khd->hqk", query_part, key_part, preferred_element_type=jnp.float32)
        * softmax_scale
    )
    row_max = jnp.max(scores, axis=-1, keepdims=True)
    weights = jnp.exp(scores - row_max)
    probs = weights / jnp.sum(weights, axis=-1, keepdims=True)
    probs_low = probs.astype(jnp.bfloat16)
    output = jnp.einsum("hqk,khd->qhd", probs_low, value_part, preferred_element_type=jnp.float32)
    delta = jnp.sum(grad_part.astype(jnp.float32) * output, axis=-1)
    dprobs = jnp.einsum("qhd,khd->hqk", grad_part, value_part, preferred_element_type=jnp.float32)
    dscores = (probs * (dprobs - jnp.transpose(delta)[:, :, None])).astype(jnp.bfloat16)
    grad_q = (
        jnp.einsum("hqk,khd->qhd", dscores, key_part, preferred_element_type=jnp.float32)
        * softmax_scale
    )
    grad_k = (
        jnp.einsum("hqk,qhd->khd", dscores, query_part, preferred_element_type=jnp.float32)
        * softmax_scale
    )
    grad_v = jnp.einsum("hqk,qhd->khd", probs_low, grad_part, preferred_element_type=jnp.float32)
    return (grad_q, grad_k, grad_v)


def general(arrays, short_offsets, global_offsets, short_stride, far_stride, n_dev):
    far_count = arrays[0].shape[0] // far_stride
    near = [pick_rows(member, short_offsets, short_stride) for member in arrays]
    split = [lax.all_to_all(m, "inner", split_axis=1, concat_axis=0, tiled=True) for m in near]
    near_grads = attend_back(*split)
    near_final = [
        lax.all_to_all(m, "inner", split_axis=0, concat_axis=1, tiled=True) for m in near_grads
    ]
    far = [pick_rows(m, global_offsets, far_stride).reshape(far_count, D) for m in arrays]
    gathered = [
        lax.all_gather(m, ("outer", "inner"), axis=0, tiled=True).reshape(KEEP_B, 4, H // 4, HD)
        for m in far
    ]
    packed = tuple(jnp.moveaxis(m, 1, 0) for m in gathered)
    mapped = lax.map(lambda pack: attend_back(*pack), packed)
    whole = [jnp.moveaxis(m, 0, 1).reshape(KEEP_B, H, HD) for m in mapped]
    start = lax.axis_index(("outer", "inner")) * far_count
    results = []
    for index in range(3):
        mine = lax.dynamic_slice_in_dim(whole[index], start, far_count, 0)
        total = put_rows(near_final[index], short_offsets, short_stride) + put_rows(
            mine, global_offsets, far_stride
        )
        results.append(total.astype(jnp.bfloat16))
    return tuple(results)


def dot(a, b, dims):
    return lax.dot_general(a, b, (dims, ((), ())), preferred_element_type=jnp.float32)


def head_back(q, k, v, g, km, qm, gm):
    scale = HD ** (-0.5)
    s = dot(km, q, ((1,), (1,)))
    m = jnp.max(s, axis=0, keepdims=True)
    w = jnp.exp2((s - m) * (scale * math.log2(math.e)))
    p = w * (1.0 / jnp.sum(w, axis=0, keepdims=True))
    pb = p.astype(jnp.bfloat16)
    dp = dot(v, gm, ((1,), (1,)))
    delta = jnp.sum(pb.astype(jnp.float32) * dp, axis=0, keepdims=True)
    ds = (p * (dp - delta)).astype(jnp.bfloat16)
    dq = dot(ds, km, ((0,), (0,))) * scale
    dk = dot(ds, qm, ((1,), (0,))) * scale
    dv = dot(pb, gm, ((1,), (0,)))
    return dq.astype(jnp.bfloat16), dk.astype(jnp.bfloat16), dv.astype(jnp.bfloat16)


def picker(count, rows, stride):
    i = lax.broadcasted_iota(jnp.int32, (count, rows), 0)
    r = lax.broadcasted_iota(jnp.int32, (count, rows), 1)
    return (r // stride == i).astype(jnp.bfloat16)


def kernel(
    n_out, n_in, stride_a, stride_b,
    x0, x1, x2, x3, offs, o0, o1, o2,
    send_a, recv_a, ret_s, ret_r, send_b, recv_b, bret_s, bret_r,
    sa_sem, ra_sem, sr_sem, rr_sem, sb_sem, rb_sem, sbr_sem, rbr_sem,
):
    xs, outs = (x0, x1, x2, x3), (o0, o1, o2)
    n_dev = n_out * n_in
    spacing = n_dev // H
    mo, me = lax.axis_index("outer"), lax.axis_index("inner")
    mine = mo * n_in + me
    rows = x0.shape[0]
    na, nb = rows // stride_a, rows // stride_b
    width = D // n_in
    tiles = width // LANES
    heads = H // n_in
    far_head = mine // spacing
    is_far = mine % spacing == 0

    def place(index):
        return (index // n_in, index % n_in)

    barrier = pltpu.get_barrier_semaphore()

    def greet(step, carry):
        pl.semaphore_signal(
            barrier, inc=1, device_id=place((mine + step) % n_dev), device_id_type=MESH
        )
        return carry

    lax.fori_loop(1, n_dev, greet, 0)

    row_of = lax.broadcasted_iota(jnp.int32, (rows, LANES), 0)
    pick_a, pick_b = picker(na, rows, stride_a), picker(nb, rows, stride_b)

    off_b = offs[1:2, :]
    rows_b = lax.broadcasted_iota(jnp.int32, (rows, D), 0) % stride_b
    mask_b = (rows_b == off_b).astype(jnp.float32).astype(jnp.bfloat16)
    for a in range(4):
        far = dot(pick_b, xs[a][...] * mask_b, ((1,), (0,))).astype(jnp.bfloat16)
        for h in range(H):
            piece = far[:, h * HD:(h + 1) * HD]
            send_b[h, a] = jnp.concatenate(
                [piece, jnp.zeros((nb, LANES - HD), jnp.bfloat16)], axis=1
            )

    pl.semaphore_wait(barrier, n_dev - 1)

    def far_copy(h):
        return pltpu.make_async_remote_copy(
            src_ref=send_b.at[h], dst_ref=recv_b.at[mine], send_sem=sb_sem.at[h],
            recv_sem=rb_sem.at[mine], device_id=place(h * spacing), device_id_type=MESH,
        )

    def far_start(h, carry):
        @pl.when(h * spacing != mine)
        def _():
            far_copy(h).start()
        return carry

    lax.fori_loop(0, H, far_start, 0)

    def near_copy(t, step):
        peer = (me + step) % n_in
        return pltpu.make_async_remote_copy(
            src_ref=send_a.at[t, peer], dst_ref=recv_a.at[t, :, me],
            send_sem=sa_sem.at[t, step - 1], recv_sem=ra_sem.at[t, step - 1],
            device_id=(mo, peer), device_id_type=MESH,
        )

    row_a = row_of % stride_a
    for t in range(tiles):
        for p in range(n_in):
            c = p * width + t * LANES
            mask = (row_a == offs[0:1, c:c + LANES]).astype(jnp.float32).astype(jnp.bfloat16)
            for a in range(4):
                send_a[t, p, a] = dot(
                    pick_a, xs[a][:, c:c + LANES] * mask, ((1,), (0,))
                ).astype(jnp.bfloat16)
        for step in range(1, n_in):
            near_copy(t, step).start()
        for a in range(4):
            recv_a[t, a, me] = send_a[t, me, a]

    def back_copy(t, step):
        peer = (me + step) % n_in
        return pltpu.make_async_remote_copy(
            src_ref=ret_s.at[t, :, peer], dst_ref=ret_r.at[t, me],
            send_sem=sr_sem.at[t, step - 1], recv_sem=rr_sem.at[t, step - 1],
            device_id=(mo, peer), device_id_type=MESH,
        )

    def near_head(i, first):
        lo, hi = i * HD, (i + 1) * HD
        t0, t1 = lo // LANES, (hi - 1) // LANES
        wide = (t1 - t0 + 1) * LANES
        lane = lax.broadcasted_iota(jnp.int32, (1, wide), 1)
        mask = ((lane >= lo - t0 * LANES) & (lane < hi - t0 * LANES)).astype(jnp.float32)
        mask = mask.astype(jnp.bfloat16)

        def whole(a):
            parts = [recv_a[t, a].reshape(n_in * na, LANES) for t in range(t0, t1 + 1)]
            return jnp.concatenate(parts, axis=1) if len(parts) > 1 else parts[0]

        q, k, v, g = (whole(a) for a in range(4))
        grads = head_back(q, k, v, g, k * mask, q * mask, g * mask)
        for index, grad in enumerate(grads):
            for t in range(t0, t1 + 1):
                part = grad[:, (t - t0) * LANES:(t - t0 + 1) * LANES]
                part = part.reshape(n_in, na, LANES)
                if t in first:
                    part = part + ret_s[t, index]
                ret_s[t, index] = part
        first.update(range(t0, t1 + 1))

    def far_wait(j, carry):
        @pl.when(j != mine)
        def _():
            pltpu.make_async_remote_copy(
                src_ref=send_b.at[0], dst_ref=recv_b.at[j], send_sem=sb_sem.at[0],
                recv_sem=rb_sem.at[j], device_id=place(j), device_id_type=MESH,
            ).wait_recv()
        return carry

    def far_back(j):
        return pltpu.make_async_remote_copy(
            src_ref=bret_s.at[j], dst_ref=bret_r.at[far_head], send_sem=sbr_sem.at[j],
            recv_sem=rbr_sem.at[far_head], device_id=place(j), device_id_type=MESH,
        )

    def far_back_start(j, carry):
        @pl.when(j != mine)
        def _():
            far_back(j).start()
        return carry

    @pl.when(is_far)
    def _():
        recv_b[mine] = send_b[far_head]
        lax.fori_loop(0, n_dev, far_wait, 0)
        q, k, v, g = (recv_b[:, a].reshape(n_dev * nb, LANES) for a in range(4))
        for index, grad in enumerate(head_back(q, k, v, g, k, q, g)):
            bret_s[:, index] = grad.reshape(n_dev, nb, LANES)
        lax.fori_loop(0, n_dev, far_back_start, 0)
        bret_r[far_head] = bret_s[mine]

    done, ready, sent = set(), 0, 0
    for i in range(heads):
        while ready * LANES < (i + 1) * HD:
            for step in range(1, n_in):
                near_copy(ready, step).wait_recv()
            ready += 1
        near_head(i, done)
        while sent < tiles and (sent + 1) * LANES <= (i + 1) * HD:
            for step in range(1, n_in):
                back_copy(sent, step).start()
            ret_r[sent, me] = ret_s[sent, :, me]
            sent += 1

    def far_back_wait(h, carry):
        @pl.when(h * spacing != mine)
        def _():
            pltpu.make_async_remote_copy(
                src_ref=bret_s.at[0], dst_ref=bret_r.at[h], send_sem=sbr_sem.at[0],
                recv_sem=rbr_sem.at[h], device_id=place(h * spacing), device_id_type=MESH,
            ).wait_recv()
            far_copy(h).wait_send()
        return carry

    lax.fori_loop(0, H, far_back_wait, 0)

    far_grads = []
    for index in range(3):
        parts = [bret_r[h, index][:, :HD] for h in range(H)]
        far_grads.append(jnp.concatenate(parts, axis=1))

    for t in range(tiles):
        for step in range(1, n_in):
            back_copy(t, step).wait_recv()
        for p in range(n_in):
            c = p * width + t * LANES
            mask = (row_a == offs[0:1, c:c + LANES]).astype(jnp.float32)
            far_mask = (row_of % stride_b == offs[1:2, c:c + LANES]).astype(jnp.float32)
            for index in range(3):
                near = dot(pick_a, ret_r[t, p, index], ((0,), (0,))) * mask
                far = dot(pick_b, far_grads[index][:, c:c + LANES], ((0,), (0,))) * far_mask
                outs[index][:, c:c + LANES] = (near + far).astype(jnp.bfloat16)

    for t in range(tiles):
        for step in range(1, n_in):
            near_copy(t, step).wait_send()
            back_copy(t, step).wait_send()

    def far_back_sent(j, carry):
        @pl.when(j != mine)
        def _():
            far_back(j).wait_send()
        return carry

    @pl.when(is_far)
    def _():
        lax.fori_loop(0, n_dev, far_back_sent, 0)


def fused(arrays, short_offsets, global_offsets, n_out, n_in, stride_a, stride_b):
    rows = arrays[0].shape[0]
    n_dev = n_out * n_in
    na, nb = rows // stride_a, rows // stride_b
    tiles = D // n_in // LANES
    offs = jnp.repeat(jnp.stack([short_offsets, global_offsets]), HD, axis=1)
    bf16 = jnp.bfloat16
    sem = pltpu.SemaphoreType.DMA
    vmem = pl.BlockSpec(memory_space=pltpu.VMEM)
    return pl.pallas_call(
        functools.partial(kernel, n_out, n_in, stride_a, stride_b),
        out_shape=[jax.ShapeDtypeStruct((rows, D), bf16)] * 3,
        in_specs=[vmem] * 5,
        out_specs=[vmem] * 3,
        scratch_shapes=[
            pltpu.VMEM((tiles, n_in, 4, na, LANES), bf16),
            pltpu.VMEM((tiles, 4, n_in, na, LANES), bf16),
            pltpu.VMEM((tiles, 3, n_in, na, LANES), bf16),
            pltpu.VMEM((tiles, n_in, 3, na, LANES), bf16),
            pltpu.VMEM((H, 4, nb, LANES), bf16),
            pltpu.VMEM((n_dev, 4, nb, LANES), bf16),
            pltpu.VMEM((n_dev, 3, nb, LANES), bf16),
            pltpu.VMEM((H, 3, nb, LANES), bf16),
            sem((tiles, n_in - 1)), sem((tiles, n_in - 1)),
            sem((tiles, n_in - 1)), sem((tiles, n_in - 1)),
            sem((H,)), sem((n_dev,)), sem((n_dev,)), sem((H,)),
        ],
        compiler_params=pltpu.CompilerParams(
            collective_id=0, has_side_effects=True, vmem_limit_bytes=56 * 1024 * 1024
        ),
    )(*arrays, offs)


def solution(mesh):
    n_out, n_in = mesh.shape["outer"], mesh.shape["inner"]

    def local(queries, key_rows, value_rows, upstream, short_offsets, global_offsets):
        arrays = (queries, key_rows, value_rows, upstream)
        rows = queries.shape[0]
        n_dev = n_out * n_in
        stride_a = rows * n_in // KEEP_A
        stride_b = rows * n_dev // KEEP_B
        fits = (rows // stride_b) % 16 == 0 and n_dev % H == 0 and D % (n_in * LANES) == 0
        if fits:
            return tuple(
                fused(arrays, short_offsets, global_offsets, n_out, n_in, stride_a, stride_b)
            )
        return general(arrays, short_offsets, global_offsets, stride_a, stride_b, n_dev)

    rows_spec = P(("outer", "inner"), None)
    return jax.shard_map(
        local, mesh=mesh, in_specs=(rows_spec,) * 4 + (P(), P()), out_specs=(rows_spec,) * 3,
        check_vma=False,
    )
```

time: 340 us -> 54 us (0.16)
  waiting for transfers between devices: 128 us -> 0 us
  local copies, waits for them, and re-layouts: 69.1 us -> 5.85 us
  matrix products: 58.6 us -> 0 us
  Pallas kernels: 0 us -> 47.3 us
  other arithmetic: 36.5 us -> 0.01 us
  starting transfers between devices: 31.7 us -> 0 us
  between operations: 14 us -> 0.67 us
    all_gather x4 -> x0, waiting for transfers between devices: 89.6 us -> none  [the longest x1 54.9 us: local(): lax.all_gather(far[1], ('outer', 'inner'), axis=0, tiled=True)]
    pallas_call x0 -> x1, Pallas kernels: none -> 47.3 us  [fused(): pl.pallas_call(functools.partial(kernel, n_out, n_in, stride_a, stride_b)...]
    all_to_all x7 -> x0, waiting for transfers between devices: 38.8 us -> none  [the longest x1 9.81 us: local(): lax.all_to_all(head_results[1], 'inner', split_axis=0, concat_axis=1, til...]
    dot_general x25 -> x0, matrix products: 37.4 us -> none  [the longest x5 10.8 us: attend_back(): jnp.einsum('hqk,khd->qhd', dscores, key_part, preferred_element_type=jnp....]
    all_to_all x7 -> x0, starting transfers between devices: 31.4 us -> none  [the longest x1 5.09 us: local(): lax.all_to_all(head_results[0], 'inner', split_axis=0, concat_axis=1, til...]
    mul x11 -> x0, local copies, waits for them, and re-layouts: 24.8 us -> none  [the longest x9 19.9 us: put_rows(): spread = grads[:, None, :, :] * onehot[None, :, :, None]]
    sub x5 -> x0, matrix products: 21.2 us -> none  [attend_back(): weights = jnp.exp(scores - row_max)]
    convert_element_type x10 -> x0, other arithmetic: 21.1 us -> none  [the longest x5 14.6 us: attend_back(): probs_low = probs.astype(jnp.bfloat16)]
  transfers between devices with their start and end apart: 11 -> 0, of which waited for: 9 -> 0; matrix products, arithmetic and copies ran while one was open for 20% -> 0% of each run, Pallas kernels for 0% -> 0%
where the time goes in v1:
time: 54 us; the launch traced here: 53.8 us
  Pallas kernels  47.3 us (88%)
  local copies, waits for them, and re-layouts  5.85 us (11%)
  between operations  0.67 us (1%)
    pallas_call x1, Pallas kernels, fused(): pl.pallas_call(functools.partial(kernel, n_out, n_in, stride_a, stride_b)...  47.3 us
    unnamed x11, local copies, waits for them, and re-layouts  5.09 us

profile of v1, /device:TPU:1, one launch (start us, length us, event | category | flops | bytes accessed | tf_op | source)
XLA Modules:
  0.0 53.8 jit_solution(249609850427192983)
XLA Ops:
  0.6 0.0 copy-start.2
  0.6 0.0 copy-start.3
  0.7 0.6 %copy-done.2 = s32[16]{0:T(128)S(1)} copy-done((s32[16]{0:T(128)S(1)}, s32[16]{0:T(128)}, u32[]{:S(2)}) %copy-start.2) | copy-done | bytes 88
  1.3 0.0 copy-done.3
  1.3 0.1 broadcast_in_dim.3
  1.4 0.7 %reshape.9.offs = s32[2,1536]{1,0:T(2,128)} reshape(s32[2,16,96]{2,1,0:T(8,128)S(1)} %broadcast_in_dim.3) | data formatting | bytes 24576 | tf_op jit(solution)/shard_map/reshape | solution.py:321
  2.1 47.3 %shard_map.85 = (bf16[256,1536]{1,0:T(8,128)(2,1)}, bf16[256,1536]{1,0:T(8,128)(2,1)}, bf16[256,1536]{1,0:T(8,128)(2,1)}) custom-call(bf16[256,1536]{1,0:T(8,128)(2,1)} %x0.1, bf16[256,1536]{1,0:T(8,128)(2,1)} %x1.1, bf16[256,1536]{1,0:T(8,128)(2,1)} %x2.1, bf16[256,1536]{1,0:T(8,128)(2,1)} %x3.1, s32[2,1536]{1,0:T(2,128)} %reshape.9.offs), custom_call_target="tpu_custom_call" | custom-call | tf_op jit(solution)/shard_map/pallas_call | solution.py:325
  49.4 0.0 copy-start.1
  49.4 2.1 %copy.12 = bf16[256,1536]{1,0:T(8,128)(2,1)} copy(bf16[256,1536]{1,0:T(8,128)(2,1)} %get-tuple-element.6) | data formatting | bytes 1572864
  51.5 0.0 copy-done.1
  51.5 0.0 copy-start
  51.5 0.9 %copy.13 = bf16[256,1536]{1,0:T(8,128)(2,1)} copy(bf16[256,1536]{1,0:T(8,128)(2,1)S(1)} %copy-done.1) | data formatting | bytes 1572864
  52.4 0.5 copy-done
  52.9 0.9 %copy.14 = bf16[256,1536]{1,0:T(8,128)(2,1)} copy(bf16[256,1536]{1,0:T(8,128)(2,1)S(1)} %copy-done) | data formatting | bytes 1572864
  (1 shorter events, 0.0 us)
Async XLA Ops:
  0.6 0.7 %copy-start.2 = (s32[16]{0:T(128)S(1)}, s32[16]{0:T(128)}, u32[]{:S(2)}) copy-start(s32[16]{0:T(128)} %param.11) | copy-start | bytes 196
  0.6 0.7 %copy-start.3 = (s32[16]{0:T(128)S(1)}, s32[16]{0:T(128)}, u32[]{:S(2)}) copy-start(s32[16]{0:T(128)} %param.10) | copy-start | bytes 196
  49.4 2.1 %copy-start.1 = (bf16[256,1536]{1,0:T(8,128)(2,1)S(1)}, bf16[256,1536]{1,0:T(8,128)(2,1)}, u32[]{:S(2)}) copy-start(bf16[256,1536]{1,0:T(8,128)(2,1)} %get-tuple-element.7) | copy-start | bytes 2359300
  51.5 1.4 %copy-start = (bf16[256,1536]{1,0:T(8,128)(2,1)S(1)}, bf16[256,1536]{1,0:T(8,128)(2,1)}, u32[]{:S(2)}) copy-start(bf16[256,1536]{1,0:T(8,128)(2,1)} %get-tuple-element.8) | copy-start | bytes 2359300

commit v2 on v1

--- a/solution.py
+++ b/solution.py
@@ -109,13 +109,31 @@
     return (r // stride == i).astype(jnp.bfloat16)
 
 
+def putter(rows, count, stride):
+    r = lax.broadcasted_iota(jnp.int32, (rows, count), 0)
+    i = lax.broadcasted_iota(jnp.int32, (rows, count), 1)
+    return (r // stride == i).astype(jnp.bfloat16)
+
+
+def lane_offsets(offsets):
+    head = lax.broadcasted_iota(jnp.int32, (1, D), 1) // HD
+    spread = jnp.zeros((1, D), jnp.int32)
+    for h in range(H):
+        spread = jnp.where(head == h, offsets[h], spread)
+    return spread
+
+
 def kernel(
     n_out, n_in, stride_a, stride_b,
-    x0, x1, x2, x3, offs, o0, o1, o2,
-    send_a, recv_a, ret_s, ret_r, send_b, recv_b, bret_s, bret_r,
-    sa_sem, ra_sem, sr_sem, rr_sem, sb_sem, rb_sem, sbr_sem, rbr_sem,
+    x0, x1, x2, x3, near_offs, far_offs, ret_r, bret_r,
+    xs, send_a, recv_a, ret_s, send_b, recv_b, bret_s,
+    in_sem, own_sem, sa_sem, ra_sem, sr_sem, rr_sem, sb_sem, rb_sem, sbr_sem, rbr_sem,
 ):
-    xs, outs = (x0, x1, x2, x3), (o0, o1, o2)
+    loads = [
+        pltpu.make_async_copy(x, xs.at[a], in_sem.at[a]) for a, x in enumerate((x0, x1, x2, x3))
+    ]
+    for load in loads:
+        load.start()
     n_dev = n_out * n_in
     spacing = n_dev // H
     mo, me = lax.axis_index("outer"), lax.axis_index("inner")
@@ -144,33 +162,6 @@
     row_of = lax.broadcasted_iota(jnp.int32, (rows, LANES), 0)
     pick_a, pick_b = picker(na, rows, stride_a), picker(nb, rows, stride_b)
 
-    off_b = offs[1:2, :]
-    rows_b = lax.broadcasted_iota(jnp.int32, (rows, D), 0) % stride_b
-    mask_b = (rows_b == off_b).astype(jnp.float32).astype(jnp.bfloat16)
-    for a in range(4):
-        far = dot(pick_b, xs[a][...] * mask_b, ((1,), (0,))).astype(jnp.bfloat16)
-        for h in range(H):
-            piece = far[:, h * HD:(h + 1) * HD]
-            send_b[h, a] = jnp.concatenate(
-                [piece, jnp.zeros((nb, LANES - HD), jnp.bfloat16)], axis=1
-            )
-
-    pl.semaphore_wait(barrier, n_dev - 1)
-
-    def far_copy(h):
-        return pltpu.make_async_remote_copy(
-            src_ref=send_b.at[h], dst_ref=recv_b.at[mine], send_sem=sb_sem.at[h],
-            recv_sem=rb_sem.at[mine], device_id=place(h * spacing), device_id_type=MESH,
-        )
-
-    def far_start(h, carry):
-        @pl.when(h * spacing != mine)
-        def _():
-            far_copy(h).start()
-        return carry
-
-    lax.fori_loop(0, H, far_start, 0)
-
     def near_copy(t, step):
         peer = (me + step) % n_in
         return pltpu.make_async_remote_copy(
@@ -179,19 +170,57 @@
             device_id=(mo, peer), device_id_type=MESH,
         )
 
+    def far_copy(h):
+        return pltpu.make_async_remote_copy(
+            src_ref=send_b.at[h], dst_ref=recv_b.at[mine], send_sem=sb_sem.at[h],
+            recv_sem=rb_sem.at[mine], device_id=place(h * spacing), device_id_type=MESH,
+        )
+
+    def far_start(h, carry):
+        @pl.when(h * spacing != mine)
+        def _():
+            far_copy(h).start()
+        return carry
+
+    off_a, off_b = lane_offsets(near_offs), lane_offsets(far_offs)
     row_a = row_of % stride_a
-    for t in range(tiles):
+
+    def pick_tile(t):
         for p in range(n_in):
             c = p * width + t * LANES
-            mask = (row_a == offs[0:1, c:c + LANES]).astype(jnp.float32).astype(jnp.bfloat16)
+            mask = (row_a == off_a[:, c:c + LANES]).astype(jnp.float32).astype(jnp.bfloat16)
             for a in range(4):
                 send_a[t, p, a] = dot(
-                    pick_a, xs[a][:, c:c + LANES] * mask, ((1,), (0,))
+                    pick_a, xs[a, :, c:c + LANES] * mask, ((1,), (0,))
                 ).astype(jnp.bfloat16)
+        for a in range(4):
+            recv_a[t, a, me] = send_a[t, me, a]
+
+    def start_tile(t):
         for step in range(1, n_in):
             near_copy(t, step).start()
-        for a in range(4):
-            recv_a[t, a, me] = send_a[t, me, a]
+
+    for load in loads:
+        load.wait()
+    pick_tile(0)
+    pl.semaphore_wait(barrier, n_dev - 1)
+    start_tile(0)
+
+    rows_b = lax.broadcasted_iota(jnp.int32, (rows, D), 0) % stride_b
+    mask_b = (rows_b == off_b).astype(jnp.float32).astype(jnp.bfloat16)
+    for a in range(4):
+        far = dot(pick_b, xs[a] * mask_b, ((1,), (0,))).astype(jnp.bfloat16)
+        for h in range(H):
+            piece = far[:, h * HD:(h + 1) * HD]
+            send_b[h, a] = jnp.concatenate(
+                [piece, jnp.zeros((nb, LANES - HD), jnp.bfloat16)], axis=1
+            )
+
+    lax.fori_loop(0, H, far_start, 0)
+
+    for t in range(1, tiles):
+        pick_tile(t)
+        start_tile(t)
 
     def back_copy(t, step):
         peer = (me + step) % n_in
@@ -245,15 +274,20 @@
             far_back(j).start()
         return carry
 
-    @pl.when(is_far)
-    def _():
+    def far_own():
+        return pltpu.make_async_copy(bret_s.at[mine], bret_r.at[far_head], own_sem.at[tiles])
+
+    def near_own(t):
+        return pltpu.make_async_copy(ret_s.at[t, :, me], ret_r.at[t, me], own_sem.at[t])
+
+    def far_whole():
         recv_b[mine] = send_b[far_head]
         lax.fori_loop(0, n_dev, far_wait, 0)
         q, k, v, g = (recv_b[:, a].reshape(n_dev * nb, LANES) for a in range(4))
         for index, grad in enumerate(head_back(q, k, v, g, k, q, g)):
             bret_s[:, index] = grad.reshape(n_dev, nb, LANES)
         lax.fori_loop(0, n_dev, far_back_start, 0)
-        bret_r[far_head] = bret_s[mine]
+        far_own().start()
 
     done, ready, sent = set(), 0, 0
     for i in range(heads):
@@ -262,10 +296,12 @@
                 near_copy(ready, step).wait_recv()
             ready += 1
         near_head(i, done)
+        if i == 0:
+            pl.when(is_far)(far_whole)
         while sent < tiles and (sent + 1) * LANES <= (i + 1) * HD:
             for step in range(1, n_in):
                 back_copy(sent, step).start()
-            ret_r[sent, me] = ret_s[sent, :, me]
+            near_own(sent).start()
             sent += 1
 
     def far_back_wait(h, carry):
@@ -280,22 +316,10 @@
 
     lax.fori_loop(0, H, far_back_wait, 0)
 
-    far_grads = []
-    for index in range(3):
-        parts = [bret_r[h, index][:, :HD] for h in range(H)]
-        far_grads.append(jnp.concatenate(parts, axis=1))
-
     for t in range(tiles):
+        near_own(t).wait()
         for step in range(1, n_in):
             back_copy(t, step).wait_recv()
-        for p in range(n_in):
-            c = p * width + t * LANES
-            mask = (row_a == offs[0:1, c:c + LANES]).astype(jnp.float32)
-            far_mask = (row_of % stride_b == offs[1:2, c:c + LANES]).astype(jnp.float32)
-            for index in range(3):
-                near = dot(pick_a, ret_r[t, p, index], ((0,), (0,))) * mask
-                far = dot(pick_b, far_grads[index][:, c:c + LANES], ((0,), (0,))) * far_mask
-                outs[index][:, c:c + LANES] = (near + far).astype(jnp.bfloat16)
 
     for t in range(tiles):
         for step in range(1, n_in):
@@ -311,6 +335,37 @@
     @pl.when(is_far)
     def _():
         lax.fori_loop(0, n_dev, far_back_sent, 0)
+        far_own().wait()
+
+
+def put_kernel(
+    stride_a, stride_b, ret_r, bret_r, near_offs, far_offs, o0, o1, o2, made, out_sem
+):
+    tiles, n_in, _, na, _ = ret_r.shape
+    nb = bret_r.shape[2]
+    rows = made.shape[1]
+    off_a, off_b = lane_offsets(near_offs), lane_offsets(far_offs)
+    row_of = lax.broadcasted_iota(jnp.int32, (rows, LANES), 0)
+    row_a, row_b = row_of % stride_a, row_of % stride_b
+    put_a = putter(rows, na, stride_a)
+    put_b = putter(rows, nb, stride_b)
+    copies = []
+    for index, out in enumerate((o0, o1, o2)):
+        parts = [bret_r[h, index][:, :HD] for h in range(H)]
+        far_grads = jnp.concatenate(parts, axis=1)
+        for t in range(tiles):
+            for p in range(n_in):
+                c = (p * tiles + t) * LANES
+                near = dot(put_a, ret_r[t, p, index], ((1,), (0,)))
+                far = dot(put_b, far_grads[:, c:c + LANES], ((1,), (0,)))
+                near = jnp.where(row_a == off_a[:, c:c + LANES], near, 0.0)
+                far = jnp.where(row_b == off_b[:, c:c + LANES], far, 0.0)
+                made[index, :, c:c + LANES] = (near + far).astype(jnp.bfloat16)
+        copy = pltpu.make_async_copy(made.at[index], out, out_sem.at[index])
+        copy.start()
+        copies.append(copy)
+    for copy in copies:
+        copy.wait()
 
 
 def fused(arrays, short_offsets, global_offsets, n_out, n_in, stride_a, stride_b):
@@ -318,32 +373,45 @@
     n_dev = n_out * n_in
     na, nb = rows // stride_a, rows // stride_b
     tiles = D // n_in // LANES
-    offs = jnp.repeat(jnp.stack([short_offsets, global_offsets]), HD, axis=1)
     bf16 = jnp.bfloat16
     sem = pltpu.SemaphoreType.DMA
     vmem = pl.BlockSpec(memory_space=pltpu.VMEM)
-    return pl.pallas_call(
+    smem = pl.BlockSpec(memory_space=pltpu.SMEM)
+    whole = pl.BlockSpec(memory_space=pl.ANY)
+    limit = 56 * 1024 * 1024
+    near, far = pl.pallas_call(
         functools.partial(kernel, n_out, n_in, stride_a, stride_b),
-        out_shape=[jax.ShapeDtypeStruct((rows, D), bf16)] * 3,
-        in_specs=[vmem] * 5,
-        out_specs=[vmem] * 3,
+        out_shape=[
+            jax.ShapeDtypeStruct((tiles, n_in, 3, na, LANES), bf16),
+            jax.ShapeDtypeStruct((H, 3, nb, LANES), bf16),
+        ],
+        in_specs=[whole] * 4 + [smem] * 2,
+        out_specs=[whole] * 2,
         scratch_shapes=[
+            pltpu.VMEM((4, rows, D), bf16),
             pltpu.VMEM((tiles, n_in, 4, na, LANES), bf16),
             pltpu.VMEM((tiles, 4, n_in, na, LANES), bf16),
             pltpu.VMEM((tiles, 3, n_in, na, LANES), bf16),
-            pltpu.VMEM((tiles, n_in, 3, na, LANES), bf16),
             pltpu.VMEM((H, 4, nb, LANES), bf16),
             pltpu.VMEM((n_dev, 4, nb, LANES), bf16),
             pltpu.VMEM((n_dev, 3, nb, LANES), bf16),
-            pltpu.VMEM((H, 3, nb, LANES), bf16),
+            sem((4,)), sem((tiles + 1,)),
             sem((tiles, n_in - 1)), sem((tiles, n_in - 1)),
             sem((tiles, n_in - 1)), sem((tiles, n_in - 1)),
             sem((H,)), sem((n_dev,)), sem((n_dev,)), sem((H,)),
         ],
         compiler_params=pltpu.CompilerParams(
-            collective_id=0, has_side_effects=True, vmem_limit_bytes=56 * 1024 * 1024
+            collective_id=0, has_side_effects=True, vmem_limit_bytes=limit
         ),
-    )(*arrays, offs)
+    )(*arrays, short_offsets, global_offsets)
+    return pl.pallas_call(
+        functools.partial(put_kernel, stride_a, stride_b),
+        out_shape=[jax.ShapeDtypeStruct((rows, D), bf16)] * 3,
+        in_specs=[vmem] * 2 + [smem] * 2,
+        out_specs=[whole] * 3,
+        scratch_shapes=[pltpu.VMEM((3, rows, D), bf16), sem((3,))],
+        compiler_params=pltpu.CompilerParams(vmem_limit_bytes=limit),
+    )(near, far, short_offsets, global_offsets)
 
 
 def solution(mesh):

time: 54 us -> 48.9 us (0.906)
  local copies, waits for them, and re-layouts: 5.85 us -> 0 us
  Pallas kernels: 47.3 us -> 48.1 us
    unnamed x11 -> x0, local copies, waits for them, and re-layouts: 5.09 us -> none
    pallas_call x0 -> x1, Pallas kernels: none -> 3.68 us  [fused(): pl.pallas_call(functools.partial(put_kernel, stride_a, stride_b), out_sha...]
    pallas_call x1, Pallas kernels: 47.3 us -> 44.5 us  [fused(): pl.pallas_call(functools.partial(kernel, n_out, n_in, stride_a, stride_b)...]
    reshape x1 -> x0, local copies, waits for them, and re-layouts: 0.69 us -> none  [fused(): offs = jnp.repeat(jnp.stack([short_offsets, global_offsets]), HD, axis=1)]
where the time goes in v2:
time: 48.9 us; the launch traced here: 48.8 us
  Pallas kernels  48.1 us (98%)
  between operations  0.64 us (1%)
    pallas_call x1, Pallas kernels, fused(): pl.pallas_call(functools.partial(kernel, n_out, n_in, stride_a, stride_b)...  44.5 us
    pallas_call x1, Pallas kernels, fused(): pl.pallas_call(functools.partial(put_kernel, stride_a, stride_b), out_sha...  3.68 us

profile of v2, /device:TPU:1, one launch (start us, length us, event | category | flops | bytes accessed | tf_op | source)
XLA Modules:
  0.0 48.8 jit_solution(5503426039238326109)
XLA Ops:
  0.6 44.5 %shard_map.85 = (bf16[3,4,3,128,128]{4,3,2,1,0:T(8,128)(2,1)}, bf16[16,3,16,128]{3,2,1,0:T(8,128)(2,1)}) custom-call(bf16[256,1536]{1,0:T(8,128)(2,1)} %x0.1, bf16[256,1536]{1,0:T(8,128)(2,1)} %x1.1, bf16[256,1536]{1,0:T(8,128)(2,1)} %x2.1, bf16[256,1536]{1,0:T(8,128)(2,1)} %x3.1, s32[16]{0:T(128)} %near_offs.3, s32[16]{0:T(128)} %far_offs.3), custom_call_target="tpu_custom_call" | custom-call | tf_op jit(solution)/shard_map/pallas_call | solution.py:382
  45.1 3.7 %shard_map.86 = (bf16[256,1536]{1,0:T(8,128)(2,1)}, bf16[256,1536]{1,0:T(8,128)(2,1)}, bf16[256,1536]{1,0:T(8,128)(2,1)}) custom-call(bf16[3,4,3,128,128]{4,3,2,1,0:T(8,128)(2,1)} %get-tuple-element.5.ret_r, bf16[16,3,16,128]{3,2,1,0:T(8,128)(2,1)} %get-tuple-element.6.bret_r, s32[16]{0:T(128)} %near_offs.3, s32[16]{0:T(128)} %far_offs.3), custom_call_target="tpu_custom_call" | custom-call | tf_op jit(solution)/shard_map/pallas_call | solution.py:407

commit v3 on v2

--- a/solution.py
+++ b/solution.py
@@ -208,13 +208,14 @@
 
     rows_b = lax.broadcasted_iota(jnp.int32, (rows, D), 0) % stride_b
     mask_b = (rows_b == off_b).astype(jnp.float32).astype(jnp.bfloat16)
+    fars = []
     for a in range(4):
         far = dot(pick_b, xs[a] * mask_b, ((1,), (0,))).astype(jnp.bfloat16)
-        for h in range(H):
-            piece = far[:, h * HD:(h + 1) * HD]
-            send_b[h, a] = jnp.concatenate(
-                [piece, jnp.zeros((nb, LANES - HD), jnp.bfloat16)], axis=1
-            )
+        fars.append(far)
+    for h in range(H):
+        packed = jnp.concatenate([far[:, h * HD:(h + 1) * HD] for far in fars], axis=1)
+        for t in range(4 * HD // LANES):
+            send_b[h, t] = packed[:, t * LANES:(t + 1) * LANES]
 
     lax.fori_loop(0, H, far_start, 0)
 
@@ -283,9 +284,13 @@
     def far_whole():
         recv_b[mine] = send_b[far_head]
         lax.fori_loop(0, n_dev, far_wait, 0)
-        q, k, v, g = (recv_b[:, a].reshape(n_dev * nb, LANES) for a in range(4))
+        packed = jnp.concatenate(
+            [recv_b[:, t].reshape(n_dev * nb, LANES) for t in range(4 * HD // LANES)], axis=1
+        )
+        q, k, v, g = (packed[:, a * HD:(a + 1) * HD] for a in range(4))
+        pad = jnp.zeros((n_dev * nb, LANES - HD), jnp.bfloat16)
         for index, grad in enumerate(head_back(q, k, v, g, k, q, g)):
-            bret_s[:, index] = grad.reshape(n_dev, nb, LANES)
+            bret_s[:, index] = jnp.concatenate([grad, pad], axis=1).reshape(n_dev, nb, LANES)
         lax.fori_loop(0, n_dev, far_back_start, 0)
         far_own().start()
 
@@ -339,9 +344,15 @@
 
 
 def put_kernel(
-    stride_a, stride_b, ret_r, bret_r, near_offs, far_offs, o0, o1, o2, made, out_sem
+    stride_a, stride_b, near_ref, bret_r, near_offs, far_offs, o0, o1, o2, ret_r, made, in_sem, out_sem
 ):
-    tiles, n_in, _, na, _ = ret_r.shape
+    tiles, n_in, _, na, _ = near_ref.shape
+    loads = [
+        pltpu.make_async_copy(near_ref.at[:, :, index], ret_r.at[index], in_sem.at[index])
+        for index in range(3)
+    ]
+    for load in loads:
+        load.start()
     nb = bret_r.shape[2]
     rows = made.shape[1]
     off_a, off_b = lane_offsets(near_offs), lane_offsets(far_offs)
@@ -353,10 +364,11 @@
     for index, out in enumerate((o0, o1, o2)):
         parts = [bret_r[h, index][:, :HD] for h in range(H)]
         far_grads = jnp.concatenate(parts, axis=1)
+        loads[index].wait()
         for t in range(tiles):
             for p in range(n_in):
                 c = (p * tiles + t) * LANES
-                near = dot(put_a, ret_r[t, p, index], ((1,), (0,)))
+                near = dot(put_a, ret_r[index, t, p], ((1,), (0,)))
                 far = dot(put_b, far_grads[:, c:c + LANES], ((1,), (0,)))
                 near = jnp.where(row_a == off_a[:, c:c + LANES], near, 0.0)
                 far = jnp.where(row_b == off_b[:, c:c + LANES], far, 0.0)
@@ -392,8 +404,8 @@
             pltpu.VMEM((tiles, n_in, 4, na, LANES), bf16),
             pltpu.VMEM((tiles, 4, n_in, na, LANES), bf16),
             pltpu.VMEM((tiles, 3, n_in, na, LANES), bf16),
-            pltpu.VMEM((H, 4, nb, LANES), bf16),
-            pltpu.VMEM((n_dev, 4, nb, LANES), bf16),
+            pltpu.VMEM((H, 4 * HD // LANES, nb, LANES), bf16),
+            pltpu.VMEM((n_dev, 4 * HD // LANES, nb, LANES), bf16),
             pltpu.VMEM((n_dev, 3, nb, LANES), bf16),
             sem((4,)), sem((tiles + 1,)),
             sem((tiles, n_in - 1)), sem((tiles, n_in - 1)),
@@ -407,9 +419,12 @@
     return pl.pallas_call(
         functools.partial(put_kernel, stride_a, stride_b),
         out_shape=[jax.ShapeDtypeStruct((rows, D), bf16)] * 3,
-        in_specs=[vmem] * 2 + [smem] * 2,
+        in_specs=[whole, vmem] + [smem] * 2,
         out_specs=[whole] * 3,
-        scratch_shapes=[pltpu.VMEM((3, rows, D), bf16), sem((3,))],
+        scratch_shapes=[
+            pltpu.VMEM((3, tiles, n_in, na, LANES), bf16),
+            pltpu.VMEM((3, rows, D), bf16), sem((3,)), sem((3,)),
+        ],
         compiler_params=pltpu.CompilerParams(vmem_limit_bytes=limit),
     )(near, far, short_offsets, global_offsets)
 

time: 48.9 us -> 49.1 us (level)
    pallas_call x1, Pallas kernels: 3.68 us -> 4.54 us  [fused(): pl.pallas_call(functools.partial(put_kernel, stride_a, stride_b), out_sha...]
    pallas_call x1, Pallas kernels: 44.5 us -> 43.8 us  [fused(): pl.pallas_call(functools.partial(kernel, n_out, n_in, stride_a, stride_b)...]
where the time goes in v3:
time: 49.1 us; the launch traced here: 48.9 us
  Pallas kernels  48.3 us (98%)
  between operations  0.64 us (1%)
    pallas_call x1, Pallas kernels, fused(): pl.pallas_call(functools.partial(kernel, n_out, n_in, stride_a, stride_b)...  43.8 us
    pallas_call x1, Pallas kernels, fused(): pl.pallas_call(functools.partial(put_kernel, stride_a, stride_b), out_sha...  4.54 us

profile of v3, /device:TPU:1, one launch (start us, length us, event | category | flops | bytes accessed | tf_op | source)
XLA Modules:
  0.0 48.9 jit_solution(2411735035762750497)
XLA Ops:
  0.6 43.8 %shard_map.85 = (bf16[3,4,3,128,128]{4,3,2,1,0:T(8,128)(2,1)}, bf16[16,3,16,128]{3,2,1,0:T(8,128)(2,1)}) custom-call(bf16[256,1536]{1,0:T(8,128)(2,1)} %x0.1, bf16[256,1536]{1,0:T(8,128)(2,1)} %x1.1, bf16[256,1536]{1,0:T(8,128)(2,1)} %x2.1, bf16[256,1536]{1,0:T(8,128)(2,1)} %x3.1, s32[16]{0:T(128)} %near_offs.3, s32[16]{0:T(128)} %far_offs.3), custom_call_target="tpu_custom_call" | custom-call | tf_op jit(solution)/shard_map/pallas_call | solution.py:394
  44.4 4.5 %shard_map.86 = (bf16[256,1536]{1,0:T(8,128)(2,1)}, bf16[256,1536]{1,0:T(8,128)(2,1)}, bf16[256,1536]{1,0:T(8,128)(2,1)}) custom-call(bf16[3,4,3,128,128]{4,3,2,1,0:T(8,128)(2,1)} %get-tuple-element.5.near_ref, bf16[16,3,16,128]{3,2,1,0:T(8,128)(2,1)} %get-tuple-element.6.bret_r, s32[16]{0:T(128)} %near_offs.3, s32[16]{0:T(128)} %far_offs.3), custom_call_target="tpu_custom_call" | custom-call | tf_op jit(solution)/shard_map/pallas_call | solution.py:419
